TPU v7x, 256 devices: a whole 4x4x8 slice. The times are simulated.
256 devices in a mesh: blk: 128 (over x, z, y_lo, core), rep: 2 (over y_hi).
Axes of the slice: x: 4, y: 4 (y_hi: 2, y_lo: 2; y = y_hi * 2 + y_lo), z: 8, core: 2. Of those that a mesh axis runs over, the one named last changes fastest.
Arguments:
- images: bfloat16 [196608, 1152], P(('rep', 'blk')), parts along dimension 0, may hold values from -0.1875 to 0.1875
- texts: bfloat16 [196608, 1152], P(('rep', 'blk')), parts along dimension 0, may hold values from -0.1875 to 0.1875
- positive: int32 [196608], P(('rep', 'blk')), parts along dimension 0, may hold values from 0 to 98303, as said below
- log_scale: float32 [2], P('rep'), parts along dimension 0, may hold values from 1.5 to 2.5
- bias: float32 [2], P('rep'), parts along dimension 0, may hold values from -4 to -2
Outputs:
- row_loss: float32 [196608], P(('rep', 'blk')), parts along dimension 0
- grad_image: float32 [196608, 1152], P(('rep', 'blk')), parts along dimension 0
- grad_text: float32 [196608, 1152], P(('rep', 'blk')), parts along dimension 0
There are 2 independent parts, one for each index of `rep`. A program takes and returns all parts, laid end to end along the dimension named above; each array names one. Nothing has to cross between parts.
Inputs may be any that keep to these rules, and one draw needn't show every extreme that they name: The positive text row of an image row of block k lies in one of the 3 text blocks k, k-1, ..., counted backwards around the 128 blocks.
All inputs are finite; a program needn't handle non-finite values.
Results may differ from a plain program's by a relative error of at most 0.0042.
Values may be sent and summed in bfloat16 or wider, within the bound.
A program may use at most 64 MiB of HBM per device.

v0:
```python
import jax
import jax.numpy as jnp
from jax import lax
from jax.sharding import PartitionSpec as P

STEPS = 3


def from_behind(block, axis, distance):
    devices = range(lax.axis_size(axis))
    route = [((i - distance) % len(devices), i) for i in devices]
    return lax.ppermute(block, axis, route)


def normalize(values):
    wide = values.astype(jnp.float32)
    inverse = lax.rsqrt(jnp.sum(wide * wide, axis=-1, keepdims=True) + 1e-06)
    return (wide * inverse, inverse)


def shards(images, texts, positive, log_scale, bias):
    row_count = images.shape[0]
    block_count = lax.axis_size("blk")
    own_index = lax.axis_index("blk")
    x_unit, x_inv = normalize(images)
    y_unit, y_inv = normalize(texts)
    x_low = x_unit.astype(jnp.bfloat16)
    y_low = y_unit.astype(jnp.bfloat16)
    logit_scale = jnp.exp(log_scale[0])
    logit_bias = bias[0]
    columns = jnp.arange(row_count, dtype=jnp.int32)
    loss_sum = jnp.zeros((row_count,), jnp.float32)
    grad_x = jnp.zeros(images.shape, jnp.float32)
    gathered_grad = jnp.zeros(images.shape, jnp.float32)
    current = y_low
    for turn_index in range(STEPS):
        if turn_index > 0:
            current = from_behind(current, "blk", 1)
        source = (own_index - turn_index) % block_count
        target = source * row_count + columns
        labels = jnp.where(positive[:, None] == target[None, :], 1.0, -1.0).astype(jnp.float32)
        logits = lax.dot_general(
            x_low, current, (((1,), (1,)), ((), ())), preferred_element_type=jnp.float32
        )
        scaled = logit_scale * logits + logit_bias
        loss_sum = loss_sum + jnp.sum(jax.nn.softplus(-labels * scaled), axis=-1)
        coefficient = (-labels * jax.nn.sigmoid(-labels * scaled)).astype(jnp.bfloat16)
        grad_x = grad_x + logit_scale * jnp.dot(
            coefficient, current, preferred_element_type=jnp.float32
        )
        text_term = logit_scale * lax.dot_general(
            coefficient, x_low, (((0,), (0,)), ((), ())), preferred_element_type=jnp.float32
        )
        if turn_index > 0:
            gathered_grad = from_behind(gathered_grad, "blk", 1) + text_term
        else:
            gathered_grad = text_term
    grad_y = from_behind(gathered_grad, "blk", -(STEPS - 1))
    grad_image = (grad_x - x_unit * jnp.sum(x_unit * grad_x, axis=-1, keepdims=True)) * x_inv
    grad_text = (grad_y - y_unit * jnp.sum(y_unit * grad_y, axis=-1, keepdims=True)) * y_inv
    row_loss = loss_sum / row_count
    return (row_loss, grad_image, grad_text)


def solution(mesh):
    in_specs = (
        P(("rep", "blk"), None),
        P(("rep", "blk"), None),
        P(("rep", "blk")),
        P("rep"),
        P("rep"),
    )
    out_specs = (P(("rep", "blk")), P(("rep", "blk"), None), P(("rep", "blk"), None))
    return jax.shard_map(shards, mesh=mesh, in_specs=in_specs, out_specs=out_specs, check_vma=False)
```

profile of v0, /device:TPU:1, one launch (start us, length us, event | category | flops | bytes accessed | tf_op | source)
XLA Modules:
  0.0 247.4 jit_solution(9838312046149070364)
XLA Ops:
  1.4 2.0 fusion.15
  3.5 1.6 fusion.2
  5.1 0.4 fusion.11
  6.3 5.2 %fusion.16 = (f32[768]{0:T(1024)}, f32[768,768]{0,1:T(8,128)S(1)}) fusion(f32[]{:T(128)} %bitcast.8, bf16[768,1152]{1,0:T(8,128)(2,1)} %fusion.2, bf16[768,1152]{1,0:T(8,128)(2,1)S(1)} %copy-done.1, f32[768]{0:T(1024)S(1)} %add_rsqrt_fusion.1, f32[]{:T(128)} %bitcast, s32[768]{0:T(1024)S(1)} %iota_add_fusion.2, s32[768]{0:T(1024)S(1)} %copy-done.4), kind=kOutput, calls=%fused_computation.28 | convolution fusion | flops 1369275648 | bytes 5910536 | tf_op jit(solution)/shard_map/dot_general | solution.py:42
  11.4 4.1 %convolution_multiply_fusion.2 = f32[768,1152]{1,0:T(8,128)} fusion(f32[]{:T(128)} %bitcast, f32[768,768]{0,1:T(8,128)S(1)} %get-tuple-element.6, s32[768]{0:T(1024)S(1)} %copy-done.4, s32[768]{0:T(1024)S(1)} %iota_add_fusion.2, bf16[768,1152]{1,0:T(8,128)(2,1)S(1)} %copy-done.1, f32[768]{0:T(1024)S(1)} %add_rsqrt_fusion.1), kind=kOutput, calls=%fused_computation.15 | convolution fusion | flops 1367212032 | bytes 7676932 | tf_op jit(solution)/shard_map/dot_general | solution.py:51
  15.5 2.7 %collective-permute-start.2 = (f32[768,1152]{1,0:T(8,128)}, f32[768,1152]{1,0:T(8,128)}, u32[]{:S(2)}, u32[]{:S(2)}) collective-permute-start(f32[768,1152]{1,0:T(8,128)} %convolution_multiply_fusion.2), channel_id=1, source_target_pairs={{254,0},{0,2},{2,4},{4,6},{6,8},{8,10},{10,12},{12,14},{14,16},{16... | collective-permute-start | bytes 10616840 | tf_op jit(solution)/shard_map/ppermute | solution.py:12
  18.2 0.0 collective-permute-start
  18.3 57.7 %collective-permute-done = bf16[768,1152]{1,0:T(8,128)(2,1)} collective-permute-done((bf16[768,1152]{1,0:T(8,128)(2,1)}, bf16[768,1152]{1,0:T(8,128)(2,1)}, u32[]{:S(2)}, u32[]{:S(2)}) %collective-permute-start) | collective-permute-done | bytes 1769504 | tf_op jit(solution)/shard_map/ppermute | solution.py:12
  75.9 5.2 %fusion.17 = (f32[768]{0:T(1024)}, f32[768,768]{0,1:T(8,128)S(1)}) fusion(f32[]{:T(128)} %bitcast.10, bf16[768,1152]{1,0:T(8,128)(2,1)} %collective-permute-done, bf16[768,1152]{1,0:T(8,128)(2,1)S(1)} %copy-done.1, f32[768]{0:T(1024)S(1)} %add_rsqrt_fusion.1, f32[]{:T(128)} %bitcast, s32[768]{0:T(1024)S(1)} %iota_add_fusion.1, s32[768]{0:T(1024)} %param.7), kind=kOutput, calls=%fused_computation.29 | convolution fusion | flops 1369275648 | bytes 5910536 | tf_op jit(solution)/shard_map/dot_general | solution.py:42
  81.2 7.0 %fusion.6 = f32[768,1152]{1,0:T(8,128)} fusion(f32[768,1152]{1,0:T(8,128)} %collective-permute-done.2, f32[]{:T(128)} %bitcast, f32[768,768]{0,1:T(8,128)S(1)} %get-tuple-element.8, s32[768]{0:T(1024)S(1)} %copy-done.5, s32[768]{0:T(1024)S(1)} %iota_add_fusion.1, bf16[768,1152]{1,0:T(8,128)(2,1)S(1)} %copy-done.1, f32[768]{0:T(1024)S(1)} %add_rsqrt_fusion.1), kind=kOutput, calls=%fused_computation.16 | convolution fusion | flops 1368096768 | bytes 11215876 | tf_op jit(solution)/shard_map/dot_general | solution.py:51
  88.1 2.5 %collective-permute-start.3 = (f32[768,1152]{1,0:T(8,128)}, f32[768,1152]{1,0:T(8,128)}, u32[]{:S(2)}, u32[]{:S(2)}) collective-permute-start(f32[768,1152]{1,0:T(8,128)} %fusion.6), channel_id=1, source_target_pairs={{254,0},{0,2},{2,4},{4,6},{6,8},{8,10},{10,12},{12,14},{14,16},{16... | collective-permute-start | bytes 10616840 | tf_op jit(solution)/shard_map/ppermute | solution.py:12
  90.7 57.7 %collective-permute-done.1 = bf16[768,1152]{1,0:T(8,128)(2,1)} collective-permute-done((bf16[768,1152]{1,0:T(8,128)(2,1)}, bf16[768,1152]{1,0:T(8,128)(2,1)}, u32[]{:S(2)}, u32[]{:S(2)}) %collective-permute-start.1) | collective-permute-done | bytes 1769504 | tf_op jit(solution)/shard_map/ppermute | solution.py:12
  148.3 4.6 %fusion.18 = (f32[768]{0:T(1024)S(1)}, f32[768,768]{0,1:T(8,128)S(1)}) fusion(f32[]{:T(128)} %bitcast.9, bf16[768,1152]{1,0:T(8,128)(2,1)} %collective-permute-done.1, bf16[768,1152]{1,0:T(8,128)(2,1)S(1)} %copy-done.1, f32[768]{0:T(1024)S(1)} %add_rsqrt_fusion.1, f32[]{:T(128)} %bitcast, s32[768]{0:T(1024)S(1)} %iota_add_fusion, s32[768]{0:T(1024)} %param.7), kind=kOutput, calls=%fused_computation.30 | convolution fusion | flops 1369275648 | bytes 5910536 | tf_op jit(solution)/shard_map/dot_general | solution.py:42
  152.9 2.3 convolution_multiply_fusion
  155.3 2.6 %add.135 = f32[768,1152]{1,0:T(8,128)S(1)} add(f32[768,1152]{1,0:T(8,128)} %collective-permute-done.3, f32[768,1152]{1,0:T(8,128)S(1)} %convolution_multiply_fusion) | non-fusion elementwise | flops 884736 | bytes 10616832 | tf_op jit(solution)/shard_map/add | solution.py:55
  157.9 11.4 %collective-permute-start.4 = (f32[768,1152]{1,0:T(8,128)S(1)}, f32[768,1152]{1,0:T(8,128)S(1)}, u32[]{:S(2)}, u32[]{:S(2)}) collective-permute-start(f32[768,1152]{1,0:T(8,128)S(1)} %add.135), channel_id=1, source_target_pairs={{4,0},{6,2},{8,4},{10,6},{12,8},{14,10},{16,12},{18,14},{20,16},{2... | collective-permute-start | bytes 10616840 | tf_op jit(solution)/shard_map/ppermute | solution.py:12
  169.3 3.4 %fusion.19 = f32[768,1152]{1,0:T(8,128)S(1)} fusion(bf16[768,1152]{1,0:T(8,128)(2,1)} %fusion.2, f32[768,768]{0,1:T(8,128)S(1)} %copy-done.10, s32[768]{0:T(1024)S(1)} %copy-done.6, s32[768]{0:T(1024)S(1)} %iota_add_fusion.2), kind=kOutput, calls=%fused_computation.46 | convolution fusion | flops 1363673088 | bytes 7673856 | tf_op jit(solution)/shard_map/dot_general | solution.py:48
  172.8 3.4 %convolution_add_fusion.1 = f32[768,1152]{1,0:T(8,128)S(1)} fusion(f32[768,1152]{1,0:T(8,128)S(1)} %fusion.19, bf16[768,1152]{1,0:T(8,128)(2,1)} %collective-permute-done, f32[768,768]{0,1:T(8,128)S(1)} %copy-done.8, s32[768]{0:T(1024)S(1)} %copy-done.6, s32[768]{0:T(1024)S(1)} %iota_add_fusion.1), kind=kOutput, calls=%fused_computation.19 | convolution fusion | flops 1364557824 | bytes 11212800 | tf_op jit(solution)/shard_map/dot_general | solution.py:48
  176.2 0.6 add_multiply_fusion.3
  176.8 4.0 %fusion.8 = (f32[768]{0:T(1024)S(1)}, f32[768,1152]{1,0:T(8,128)S(1)}) fusion(bf16[768,1152]{1,0:T(8,128)(2,1)S(1)} %copy-done.1, f32[768]{0:T(1024)S(1)} %add_rsqrt_fusion.1, f32[]{:T(128)} %bitcast, f32[768,1152]{1,0:T(8,128)S(1)} %convolution_add_fusion.1, bf16[768,1152]{1,0:T(8,128)(2,1)} %collective-permute-done.1, ...), kind=kOutput, calls=%fused_computation.20 | convolution fusion | flops 1368980736 | bytes 12988420 | tf_op jit(solution)/shard_map/dot_general | solution.py:48
  180.8 2.5 %fusion.10 = f32[768,1152]{1,0:T(8,128)} fusion(f32[768,1152]{1,0:T(8,128)S(1)} %get-tuple-element.10, bf16[768,1152]{1,0:T(8,128)(2,1)S(1)} %copy-done.1, f32[768]{0:T(1024)S(1)} %get-tuple-element.9, f32[768]{0:T(1024)S(1)} %add_rsqrt_fusion.1), kind=kLoop, calls=%fused_computation.22 | loop fusion | flops 4423680 | bytes 8853504 | tf_op jit(solution)/shard_map/mul | solution.py:59
  183.3 61.1 %collective-permute-done.4 = f32[768,1152]{1,0:T(8,128)S(1)} collective-permute-done((f32[768,1152]{1,0:T(8,128)S(1)}, f32[768,1152]{1,0:T(8,128)S(1)}, u32[]{:S(2)}, u32[]{:S(2)}) %collective-permute-start.4) | collective-permute-done | bytes 3538976 | tf_op jit(solution)/shard_map/ppermute | solution.py:12
  244.3 0.7 fusion.12
  245.0 2.5 fusion.14
  (30 shorter events, 0.1 us)
Async XLA Ops:
  0.6 2.8 %copy-start = (bf16[768,1152]{1,0:T(8,128)(2,1)S(1)}, bf16[768,1152]{1,0:T(8,128)(2,1)}, u32[]{:S(2)}) copy-start(bf16[768,1152]{1,0:T(8,128)(2,1)} %param.6) | copy-start | bytes 5308420
  1.4 3.7 %copy-start.1 = (bf16[768,1152]{1,0:T(8,128)(2,1)S(1)}, bf16[768,1152]{1,0:T(8,128)(2,1)}, u32[]{:S(2)}) copy-start(bf16[768,1152]{1,0:T(8,128)(2,1)} %param.5) | copy-start | bytes 5308420
  3.5 2.8 %copy-start.4 = (s32[768]{0:T(1024)S(1)}, s32[768]{0:T(1024)}, u32[]{:S(2)}) copy-start(s32[768]{0:T(1024)} %param.7) | copy-start | bytes 9220
  11.4 4.1 %copy-start.9 = (f32[768,768]{0,1:T(8,128)}, f32[768,768]{0,1:T(8,128)S(1)}, u32[]{:S(2)}) copy-start(f32[768,768]{0,1:T(8,128)S(1)} %get-tuple-element.6) | copy-start | bytes 7077892
  15.5 65.6 %collective-permute-start.2 = (f32[768,1152]{1,0:T(8,128)}, f32[768,1152]{1,0:T(8,128)}, u32[]{:S(2)}, u32[]{:S(2)}) collective-permute-start(f32[768,1152]{1,0:T(8,128)} %convolution_multiply_fusion.2), channel_id=1, source_target_pairs={{254,0},{0,2},{2,4},{4,6},{6,8},{8,10},{10,12},{12,14},{14,16},{16... | collective-permute-start | bytes 10616840 | tf_op jit(solution)/shard_map/ppermute | solution.py:12
  18.2 57.7 %collective-permute-start = (bf16[768,1152]{1,0:T(8,128)(2,1)}, bf16[768,1152]{1,0:T(8,128)(2,1)}, u32[]{:S(2)}, u32[]{:S(2)}) collective-permute-start(bf16[768,1152]{1,0:T(8,128)(2,1)} %fusion.2), channel_id=1, source_target_pairs={{254,0},{0,2},{2,4},{4,6},{6,8},{8,10},{10,12},{12,14},{14,16},{16... | collective-permute-start | bytes 5308424 | tf_op jit(solution)/shard_map/ppermute | solution.py:12
  75.9 5.2 %copy-start.5 = (s32[768]{0:T(1024)S(1)}, s32[768]{0:T(1024)}, u32[]{:S(2)}) copy-start(s32[768]{0:T(1024)} %param.7) | copy-start | bytes 9220
  81.1 7.0 %copy-start.7 = (f32[768,768]{0,1:T(8,128)}, f32[768,768]{0,1:T(8,128)S(1)}, u32[]{:S(2)}) copy-start(f32[768,768]{0,1:T(8,128)S(1)} %get-tuple-element.8) | copy-start | bytes 7077892
  88.1 67.1 %collective-permute-start.3 = (f32[768,1152]{1,0:T(8,128)}, f32[768,1152]{1,0:T(8,128)}, u32[]{:S(2)}, u32[]{:S(2)}) collective-permute-start(f32[768,1152]{1,0:T(8,128)} %fusion.6), channel_id=1, source_target_pairs={{254,0},{0,2},{2,4},{4,6},{6,8},{8,10},{10,12},{12,14},{14,16},{16... | collective-permute-start | bytes 10616840 | tf_op jit(solution)/shard_map/ppermute | solution.py:12
  90.6 57.7 %collective-permute-start.1 = (bf16[768,1152]{1,0:T(8,128)(2,1)}, bf16[768,1152]{1,0:T(8,128)(2,1)}, u32[]{:S(2)}, u32[]{:S(2)}) collective-permute-start(bf16[768,1152]{1,0:T(8,128)(2,1)} %collective-permute-done), channel_id=1, source_target_pairs={{254,0},{0,2},{2,4},{4,6},{6,8},{8,10},{10,12},{12,14},{14,16},{16... | collective-permute-start | bytes 5308424 | tf_op jit(solution)/shard_map/ppermute | solution.py:12
  148.3 4.6 %copy-start.6 = (s32[768]{0:T(1024)S(1)}, s32[768]{0:T(1024)}, u32[]{:S(2)}) copy-start(s32[768]{0:T(1024)} %param.7) | copy-start | bytes 9220
  155.3 14.1 %copy-start.10 = (f32[768,768]{0,1:T(8,128)S(1)}, f32[768,768]{0,1:T(8,128)}, u32[]{:S(2)}) copy-start(f32[768,768]{0,1:T(8,128)} %copy-done.9) | copy-start | bytes 7077892
  157.9 14.9 %copy-start.8 = (f32[768,768]{0,1:T(8,128)S(1)}, f32[768,768]{0,1:T(8,128)}, u32[]{:S(2)}) copy-start(f32[768,768]{0,1:T(8,128)} %copy-done.7) | copy-start | bytes 7077892
  157.9 86.4 %collective-permute-start.4 = (f32[768,1152]{1,0:T(8,128)S(1)}, f32[768,1152]{1,0:T(8,128)S(1)}, u32[]{:S(2)}, u32[]{:S(2)}) collective-permute-start(f32[768,1152]{1,0:T(8,128)S(1)} %add.135), channel_id=1, source_target_pairs={{4,0},{6,2},{8,4},{10,6},{12,8},{14,10},{16,12},{18,14},{20,16},{2... | collective-permute-start | bytes 10616840 | tf_op jit(solution)/shard_map/ppermute | solution.py:12
  172.8 3.4 %copy-start.2 = (f32[768]{0:T(1024)S(1)}, f32[768]{0:T(1024)}, u32[]{:S(2)}) copy-start(f32[768]{0:T(1024)} %get-tuple-element.5) | copy-start | bytes 9220
  172.8 3.4 %copy-start.3 = (f32[768]{0:T(1024)S(1)}, f32[768]{0:T(1024)}, u32[]{:S(2)}) copy-start(f32[768]{0:T(1024)} %get-tuple-element.7) | copy-start | bytes 9220
where the time goes:
time: 248 us; the launch traced here: 247 us
  waiting for transfers between devices  176 us (71%)
  matrix products  39.2 us (16%)
  starting transfers between devices  16.7 us (7%)
  other arithmetic  12.9 us (5%)
    ppermute x5, waiting for transfers between devices, from_behind(): return lax.ppermute(block, axis, route)  176 us
    ppermute x5, starting transfers between devices, from_behind(): return lax.ppermute(block, axis, route)  16.7 us
    dot_general x3, matrix products, shards(): lax.dot_general(x_low, current, (((1,), (1,)), ((), ())), preferred_eleme...  15 us
    dot_general x3, matrix products, shards(): lax.dot_general(coefficient, x_low, (((0,), (0,)), ((), ())), preferred_e...  13.4 us
    dot_general x3, matrix products, shards(): jnp.dot(coefficient, current, preferred_element_type=jnp.float32)  10.8 us
  transfers between devices with their start and end apart: 5, of which 3 were waited for; matrix products, arithmetic and copies ran while one was open for 10% of the time, Pallas kernels for 0%

commit v1 on v0

v1 whole, which is shorter than its diff:
```python
import functools

import jax
import jax.numpy as jnp
from jax import lax
from jax.experimental import pallas as pl
from jax.experimental.pallas import tpu as pltpu
from jax.sharding import PartitionSpec as P

STEPS = 3
CHUNK = 128
MESH = pl.DeviceIdType.MESH


def kernel(
    scale_ref, bias_ref, pos_ref, img_ref, txt_ref,
    loss_ref, gx_ref, gy_ref,
    xraw, yraw, xl, yl, xinv, yinv, t1, t2, i1, i2, pos1, pos2, posb, loss_acc,
    load_sem, link_t_s, link_t_r, link_i_s, link_i_r, d2d_t_s, d2d_t_r, d2d_i_s, d2d_i_r,
    pos_s, pos_r,
):
    rows, width = xraw.shape
    chunks = rows // CHUNK
    n = lax.axis_size("blk")
    me = lax.axis_index("blk")
    core = lax.rem(me, 2)
    ahead = lax.rem(me + 2, n)
    behind = lax.rem(me + n - 2, n)
    partner = me + 1 - 2 * core
    first = core == 0
    second = core == 1

    barrier = pltpu.get_barrier_semaphore()
    for other in (ahead, behind, partner):
        pl.semaphore_signal(barrier, inc=1, device_id={"blk": other}, device_id_type=MESH)

    def part(c):
        return pl.ds(pl.multiple_of(c * CHUNK, CHUNK), CHUNK)

    load_x = pltpu.make_async_copy(img_ref, xraw, load_sem.at[0])
    load_y = pltpu.make_async_copy(txt_ref, yraw, load_sem.at[1])
    load_y.start()
    load_x.start()

    def normalize(raw, low, inv):
        def step(c, carry):
            wide = raw[part(c), :].astype(jnp.float32)
            inverse = lax.rsqrt(jnp.sum(wide * wide, axis=-1, keepdims=True) + 1e-06)
            inv[part(c), :] = jnp.broadcast_to(inverse, (CHUNK, 128))
            low[part(c), :] = (wide * inverse).astype(jnp.bfloat16)
            return carry

        lax.fori_loop(0, chunks, step, 0)

    load_y.wait()
    normalize(yraw, yl, yinv)
    load_x.wait()
    normalize(xraw, xl, xinv)

    def link_t(c):
        return pltpu.make_async_remote_copy(
            src_ref=yl.at[part(c)], dst_ref=t2.at[part(c)], send_sem=link_t_s.at[c], recv_sem=link_t_r.at[c],
            device_id={"blk": ahead}, device_id_type=MESH)

    def link_i(c):
        return pltpu.make_async_remote_copy(
            src_ref=xl.at[part(c)], dst_ref=i2.at[part(c)], send_sem=link_i_s.at[c], recv_sem=link_i_r.at[c],
            device_id={"blk": behind}, device_id_type=MESH)

    def d2d_t(c, source):
        return pltpu.make_async_remote_copy(
            src_ref=source.at[part(c)], dst_ref=t1.at[part(c)], send_sem=d2d_t_s.at[c], recv_sem=d2d_t_r.at[c],
            device_id={"blk": partner}, device_id_type=MESH)

    def d2d_i(c, source):
        return pltpu.make_async_remote_copy(
            src_ref=source.at[part(c)], dst_ref=i1.at[part(c)], send_sem=d2d_i_s.at[c], recv_sem=d2d_i_r.at[c],
            device_id={"blk": partner}, device_id_type=MESH)

    pos_link = pltpu.make_async_remote_copy(
        src_ref=pos_ref, dst_ref=pos2, send_sem=pos_s.at[0], recv_sem=pos_r.at[0],
        device_id={"blk": behind}, device_id_type=MESH)

    def pos_d2d(source):
        return pltpu.make_async_remote_copy(
            src_ref=source, dst_ref=pos1, send_sem=pos_s.at[1], recv_sem=pos_r.at[1],
            device_id={"blk": partner}, device_id_type=MESH)

    pl.semaphore_wait(barrier, 3)
    pos_link.start()

    def start_t(c, carry):
        link_t(c).start()
        return carry

    def start_i(c, carry):
        link_i(c).start()
        return carry

    lax.fori_loop(0, chunks, start_t, 0)
    lax.fori_loop(0, chunks, start_i, 0)

    @pl.when(first)
    def _():
        def go(c, carry):
            d2d_t(c, yl).start()
            return carry

        lax.fori_loop(0, chunks, go, 0)

    @pl.when(second)
    def _():
        pos_d2d(pos_ref).start()

        def go(c, carry):
            d2d_i(c, xl).start()
            return carry

        lax.fori_loop(0, chunks, go, 0)

    scale = jnp.exp(jnp.full((8, 128), scale_ref[0], jnp.float32))[0:1]
    bias = jnp.full((1, 128), bias_ref[0], jnp.float32)
    gx_ref[...] = jnp.zeros_like(gx_ref)
    gy_ref[...] = jnp.zeros_like(gy_ref)
    loss_acc[...] = jnp.zeros_like(loss_acc)

    def spread(c, carry):
        row = pos_ref[pl.ds(c, 1), :].astype(jnp.float32)
        posb[part(c), :] = jnp.broadcast_to(row, (CHUNK, CHUNK)).T
        return carry

    lax.fori_loop(0, chunks, spread, 0)

    lanes = lax.broadcasted_iota(jnp.int32, (CHUNK, CHUNK), 1)
    subs = lax.broadcasted_iota(jnp.int32, (CHUNK, CHUNK), 0)

    def text_chunk(block, source, c):
        base = (source * rows + c * CHUNK + lanes).astype(jnp.float32)

        def tile(r, carry):
            logits = lax.dot_general(
                xl[part(r), :], block[part(c), :], (((1,), (1,)), ((), ())), preferred_element_type=jnp.float32)
            scaled = scale * logits + bias
            match = posb[part(r), :] == base
            z = jnp.where(match, -scaled, scaled)
            e = jnp.exp(-jnp.abs(z))
            loss_acc[part(r), :] += jnp.maximum(z, 0.0) + jnp.log1p(e)
            s = jnp.where(z >= 0, 1.0, e) / (1.0 + e)
            coefficient = jnp.where(match, -s, s).astype(jnp.bfloat16)
            gx_ref[part(r), :] += jnp.dot(coefficient, block[part(c), :], preferred_element_type=jnp.float32)
            return carry

        lax.fori_loop(0, chunks, tile, 0)

    def image_chunk(block, positions, c):
        pos_row = positions[pl.ds(c, 1), :]

        def tile(r, carry):
            logits = lax.dot_general(
                yl[part(r), :], block[part(c), :], (((1,), (1,)), ((), ())), preferred_element_type=jnp.float32)
            scaled = scale * logits + bias
            match = pos_row == (me * rows + r * CHUNK + subs)
            z = jnp.where(match, -scaled, scaled)
            s = 1.0 / (1.0 + jnp.exp(-z))
            coefficient = jnp.where(match, -s, s).astype(jnp.bfloat16)
            gy_ref[part(r), :] += jnp.dot(coefficient, block[part(c), :], preferred_element_type=jnp.float32)
            return carry

        lax.fori_loop(0, chunks, tile, 0)

    def own(c, carry):
        text_chunk(yl, me, c)
        image_chunk(xl, pos_ref, c)
        return carry

    lax.fori_loop(0, chunks, own, 0)

    def texts_in(c, carry):
        link_t(c).wait_recv()

        @pl.when(second)
        def _():
            d2d_t(c, t2).start()

        text_chunk(t2, lax.rem(me + n - 2, n), c)
        d2d_t(c, yl).wait_recv()
        text_chunk(t1, lax.rem(me + n - 1, n), c)
        return carry

    lax.fori_loop(0, chunks, texts_in, 0)

    def finish(acc, raw, inv):
        def step(c, carry):
            unit = raw[part(c), :].astype(jnp.float32) * inv[part(c), 0:1]
            grad = acc[part(c), :] * scale[0:1, 0:1]
            dot = jnp.sum(unit * grad, axis=-1, keepdims=True)
            acc[part(c), :] = (grad - unit * dot) * inv[part(c), 0:1]
            return carry

        lax.fori_loop(0, chunks, step, 0)

    finish(gx_ref, xraw, xinv)

    def losses(c, carry):
        total = jnp.sum(loss_acc[part(c), :].T, axis=0, keepdims=True)
        loss_ref[pl.ds(c, 1), :] = total / rows
        return carry

    lax.fori_loop(0, chunks, losses, 0)

    pos_link.wait_recv()

    @pl.when(first)
    def _():
        pos_d2d(pos2).start()

    def images_in(c, carry):
        link_i(c).wait_recv()

        @pl.when(first)
        def _():
            d2d_i(c, i2).start()

        image_chunk(i2, pos2, c)

        @pl.when(c == 0)
        def _():
            pos_d2d(pos_ref).wait_recv()

        d2d_i(c, xl).wait_recv()
        image_chunk(i1, pos1, c)
        return carry

    lax.fori_loop(0, chunks, images_in, 0)
    finish(gy_ref, yraw, yinv)

    pos_link.wait_send()
    pos_d2d(pos_ref).wait_send()

    def drain(c, carry):
        link_t(c).wait_send()
        link_i(c).wait_send()
        d2d_t(c, yl).wait_send()
        d2d_i(c, xl).wait_send()
        return carry

    lax.fori_loop(0, chunks, drain, 0)


def shards(images, texts, positive, log_scale, bias):
    rows, width = images.shape
    chunks = rows // CHUNK
    low = pltpu.VMEM((rows, width), jnp.bfloat16)
    column = pltpu.VMEM((rows, 128), jnp.float32)
    places = pltpu.VMEM((chunks, CHUNK), jnp.int32)
    sems = pltpu.SemaphoreType.DMA((chunks,))
    pair = pltpu.SemaphoreType.DMA((2,))
    vmem = pl.BlockSpec(memory_space=pltpu.VMEM)
    smem = pl.BlockSpec(memory_space=pltpu.SMEM)
    hbm = pl.BlockSpec(memory_space=pl.ANY)
    loss, grad_x, grad_y = pl.pallas_call(
        kernel,
        out_shape=(
            jax.ShapeDtypeStruct((chunks, CHUNK), jnp.float32),
            pltpu.VMEM((rows, width), jnp.float32),
            pltpu.VMEM((rows, width), jnp.float32),
        ),
        in_specs=[smem, smem, vmem, hbm, hbm],
        out_specs=(vmem, vmem, vmem),
        scratch_shapes=[low] * 4 + [column] * 2 + [low] * 4 + [places] * 2 + [column] * 2 + [pair] + [sems] * 8 + [pair] * 2,
        compiler_params=pltpu.CompilerParams(
            collective_id=0, has_side_effects=True, vmem_limit_bytes=40 * 2**20),
    )(log_scale, bias, positive.reshape(chunks, CHUNK), images, texts)
    return (loss.reshape(rows), grad_x, grad_y)


def solution(mesh):
    in_specs = (
        P(("rep", "blk"), None),
        P(("rep", "blk"), None),
        P(("rep", "blk")),
        P("rep"),
        P("rep"),
    )
    out_specs = (P(("rep", "blk")), P(("rep", "blk"), None), P(("rep", "blk"), None))
    return jax.shard_map(shards, mesh=mesh, in_specs=in_specs, out_specs=out_specs, check_vma=False)
```

time: 248 us -> 145 us (0.58)
  waiting for transfers between devices: 176 us -> 0 us
  Pallas kernels: 0 us -> 135 us
  matrix products: 39.2 us -> 0 us
  starting transfers between devices: 16.7 us -> 0 us
  other arithmetic: 12.9 us -> 0 us
  local copies, waits for them, and re-layouts: 0.05 us -> 7.81 us
    ppermute x5 -> x0, waiting for transfers between devices: 176 us -> none  [from_behind(): return lax.ppermute(block, axis, route)]
    pallas_call x0 -> x1, Pallas kernels: none -> 135 us  [shards(): pl.pallas_call(kernel, out_shape=(jax.ShapeDtypeStruct((chunks, CHUNK), j...]
    dot_general x9 -> x0, matrix products: 39.2 us -> none  [the longest x3 15 us: shards(): lax.dot_general(x_low, current, (((1,), (1,)), ((), ())), preferred_eleme...]
    ppermute x5 -> x0, starting transfers between devices: 16.7 us -> none  [from_behind(): return lax.ppermute(block, axis, route)]
    unnamed x22 -> x9, local copies, waits for them, and re-layouts: 0.05 us -> 7.81 us
    mul x2 -> x0, other arithmetic: 4.95 us -> none  [the longest x1 2.48 us: shards(): (grad_x - x_unit * jnp.sum(x_unit * grad_x, axis=-1, keepdims=True)) * x_inv]
    reduce_sum x3 -> x0, other arithmetic: 3.08 us -> none  [the longest x2 2.43 us: normalize(): inverse = lax.rsqrt(jnp.sum(wide * wide, axis=-1, keepdims=True) + 1e-06)]
    add x4 -> x0, other arithmetic: 2.62 us -> none  [the longest x1 2.61 us: shards(): gathered_grad = from_behind(gathered_grad, 'blk', 1) + text_term]
  transfers between devices with their start and end apart: 5 -> 0, of which waited for: 3 -> 0; matrix products, arithmetic and copies ran while one was open for 10% -> 0% of each run, Pallas kernels for 0% -> 0%
where the time goes in v1:
time: 145 us
  Pallas kernels  135 us (93%)
  local copies, waits for them, and re-layouts  7.81 us (5%)
  between operations  1.94 us (1%)
    pallas_call x1, Pallas kernels, shards(): pl.pallas_call(kernel, out_shape=(jax.ShapeDtypeStruct((chunks, CHUNK), j...  135 us
    unnamed x9, local copies, waits for them, and re-layouts  7.81 us

profile of v1, /device:TPU:1, one launch (start us, length us, event | category | flops | bytes accessed | tf_op | source)
XLA Modules:
  0.0 144.9 jit_solution(8188515275878529829)
XLA Ops:
  1.9 0.0 copy-start
  1.9 1.5 %copy-done = bf16[768,1152]{1,0:T(8,128)(2,1)S(1)} copy-done((bf16[768,1152]{1,0:T(8,128)(2,1)S(1)}, bf16[768,1152]{1,0:T(8,128)(2,1)}, u32[]{:S(2)}) %copy-start) | copy-done | bytes 1769496
  3.4 0.0 copy-start.1
  3.4 1.5 %copy-done.1 = bf16[768,1152]{1,0:T(8,128)(2,1)S(1)} copy-done((bf16[768,1152]{1,0:T(8,128)(2,1)S(1)}, bf16[768,1152]{1,0:T(8,128)(2,1)}, u32[]{:S(2)}) %copy-start.1) | copy-done | bytes 1769496
  4.9 0.0 copy-start.2
  4.9 0.7 copy-done.2
  5.6 135.1 %shard_map.76 = (f32[6,128]{1,0:T(8,128)S(1)}, f32[768,1152]{1,0:T(8,128)S(1)}, f32[768,1152]{1,0:T(8,128)S(1)}) custom-call(f32[1]{0:T(128)S(6)} %copy.13.scale_ref, f32[1]{0:T(128)S(6)} %copy.14.bias_ref, s32[6,128]{1,0:T(8,128)S(1)} %bitcast.2, bf16[768,1152]{1,0:T(8,128)(2,1)S(1)} %copy-done, bf16[768,1152]{1,0:T(8,128)(2,1)S(1)} %copy-done.1), custom_call_target="tpu_custom_call" | custom-call | tf_op jit(solution)/shard_map/pallas_call | solution.py:261
  140.7 1.8 %copy.11 = f32[768,1152]{1,0:T(8,128)} copy(f32[768,1152]{1,0:T(8,128)S(1)} %get-tuple-element.10) | data formatting | bytes 7077888
  142.5 1.8 %copy.12 = f32[768,1152]{1,0:T(8,128)} copy(f32[768,1152]{1,0:T(8,128)S(1)} %get-tuple-element.11) | data formatting | bytes 7077888
  144.3 0.6 copy.15
Async XLA Ops:
  1.9 1.5 %copy-start = (bf16[768,1152]{1,0:T(8,128)(2,1)S(1)}, bf16[768,1152]{1,0:T(8,128)(2,1)}, u32[]{:S(2)}) copy-start(bf16[768,1152]{1,0:T(8,128)(2,1)} %img_ref.1) | copy-start | bytes 5308420
  3.4 1.5 %copy-start.1 = (bf16[768,1152]{1,0:T(8,128)(2,1)S(1)}, bf16[768,1152]{1,0:T(8,128)(2,1)}, u32[]{:S(2)}) copy-start(bf16[768,1152]{1,0:T(8,128)(2,1)} %txt_ref.1) | copy-start | bytes 5308420
  4.9 0.7 copy-start.2

commit v2 on v0

v2 whole, which is shorter than its diff:
```python
import functools

import jax
import jax.numpy as jnp
from jax import lax
from jax.experimental import pallas as pl
from jax.experimental.pallas import tpu as pltpu
from jax.sharding import PartitionSpec as P

PART = 128
TILE = 256
LAST_TILE = 256
IN_FLIGHT = 4
MESH = pl.DeviceIdType.MESH
IMAGE, TEXT = 0, 1
FAR, NEAR = 0, 1


def at_rows(start, size):
    return pl.ds(pl.multiple_of(start, size), size)


def kernel(
    scale_hbm, bias_hbm, pos_hbm, img_ref, txt_ref,
    loss_ref, gx_ref, gy_ref,
    scale_ref, bias_ref, pos_ref, raw, low, inv, there, places, posb, loss_acc,
    load_sem, lead_s, lead_r, tail_s, tail_r, pass_s, pass_r, whole_s, whole_r, pos_s, pos_r,
):
    _, rows, width = raw.shape
    parts = rows // PART
    tiles = rows // TILE
    n = lax.axis_size("blk")
    me = lax.axis_index("blk")
    core = lax.rem(me, 2)
    other = 1 - core
    ahead = lax.rem(me + 2, n)
    behind = lax.rem(me + n - 2, n)
    partner = me + 1 - 2 * core
    first = core == 0
    second = core == 1

    barrier = pltpu.get_barrier_semaphore()
    for device in (ahead, behind, partner):
        pl.semaphore_signal(barrier, inc=1, device_id={"blk": device}, device_id_type=MESH)

    loads = [
        pltpu.make_async_copy(img_ref, raw.at[IMAGE], load_sem.at[0]),
        pltpu.make_async_copy(txt_ref, raw.at[TEXT], load_sem.at[1]),
        pltpu.make_async_copy(pos_hbm, pos_ref, load_sem.at[2]),
        pltpu.make_async_copy(scale_hbm, scale_ref, load_sem.at[3]),
        pltpu.make_async_copy(bias_hbm, bias_ref, load_sem.at[4]),
    ]
    for load in loads:
        load.start()

    def remote(source, target, sent, got, device):
        return pltpu.make_async_remote_copy(
            src_ref=source, dst_ref=target, send_sem=sent, recv_sem=got,
            device_id={"blk": device}, device_id_type=MESH)

    def lead(c):
        r = at_rows(c * PART, PART)
        return remote(low.at[core, r], there.at[core, FAR, r], lead_s.at[c], lead_r.at[c],
                      jnp.where(first, behind, ahead))

    def tail(c):
        r = at_rows(c * PART, PART)
        return remote(low.at[other, r], there.at[other, FAR, r], tail_s.at[c], tail_r.at[c],
                      jnp.where(first, ahead, behind))

    def pass_on(c):
        r = at_rows(c * PART, PART)
        return remote(there.at[core, FAR, r], there.at[core, NEAR, r], pass_s.at[c], pass_r.at[c], partner)

    whole = remote(low.at[other], there.at[other, NEAR], whole_s.at[0], whole_r.at[0], partner)
    pos_link = remote(pos_ref, places.at[FAR], pos_s.at[0], pos_r.at[0], behind)

    def pos_near(source):
        return remote(source, places.at[NEAR], pos_s.at[1], pos_r.at[1], partner)

    def normalize(kind):
        def step(c, carry):
            r = at_rows(c * PART, PART)
            wide = raw[kind, r, :].astype(jnp.float32)
            inverse = lax.rsqrt(jnp.sum(wide * wide, axis=-1, keepdims=True) + 1e-06)
            inv[kind, r, :] = jnp.broadcast_to(inverse, (PART, 128))
            low[kind, r, :] = (wide * inverse).astype(jnp.bfloat16)
            return carry

        lax.fori_loop(0, parts, step, 0)

    loads[0].wait()
    normalize(IMAGE)
    loads[1].wait()
    normalize(TEXT)
    for load in loads[2:]:
        load.wait()

    pl.semaphore_wait(barrier, 3)
    def start(p):
        is_tail = jnp.logical_or(p == 2 * parts - 1, jnp.logical_and(p > 0, lax.rem(p, 2) == 0))

        @pl.when(jnp.logical_and(p < 2 * parts, is_tail))
        def _():
            tail(lax.div(p - 1, 2)).start()

        @pl.when(jnp.logical_and(p < 2 * parts, jnp.logical_not(is_tail)))
        def _():
            lead(lax.div(p + 1, 2)).start()

    def fill(p, carry):
        start(p)
        return carry

    pos_link.start()

    @pl.when(second)
    def _():
        pos_near(pos_ref).start()

    whole.start()
    lax.fori_loop(0, IN_FLIGHT, fill, 0)

    scale = jnp.exp(jnp.full((8, 128), scale_ref[0], jnp.float32))[0:1, 0:1]
    bias = bias_ref[0]

    def spread(c, carry):
        row = pos_ref[pl.ds(c, 1), :].astype(jnp.float32)
        posb[at_rows(c * 128, 128), :] = jnp.broadcast_to(row, (128, 128)).T
        return carry

    lax.fori_loop(0, rows // 128, spread, 0)

    def logits_of(own, block):
        dots = lax.dot_general(own, block, (((1,), (1,)), ((), ())), preferred_element_type=jnp.float32)
        return scale * dots + bias

    def text_terms(at, block, target, wide):
        scaled = logits_of(low[IMAGE, at, :], block)
        match = jnp.concatenate([posb[at, :]] * (wide // 128), axis=1) == target
        z = jnp.where(match, -scaled, scaled)
        e = jnp.exp(-jnp.abs(z))
        term = jnp.maximum(z, 0.0) + jnp.log1p(e)
        s = jnp.where(z >= 0, 1.0, e) / (1.0 + e)
        coefficient = jnp.where(match, -s, s).astype(jnp.bfloat16)
        loss = functools.reduce(jnp.add, [term[:, g:g + 128] for g in range(0, wide, 128)])
        return loss, jnp.dot(coefficient, block, preferred_element_type=jnp.float32)

    def image_terms(at, start, size, block, pos_row):
        scaled = logits_of(low[TEXT, at, :], block)
        subs = lax.broadcasted_iota(jnp.int32, scaled.shape, 0)
        match = pos_row == me * rows + start + subs
        z = jnp.where(match, -scaled, scaled)
        s = 1.0 / (1.0 + jnp.exp(-z))
        coefficient = jnp.where(match, -s, s).astype(jnp.bfloat16)
        return jnp.dot(coefficient, block, preferred_element_type=jnp.float32)

    def targets(source, start, size, wide):
        lanes = lax.broadcasted_iota(jnp.int32, (size, wide), 1)
        return (source * rows + start + lanes).astype(jnp.float32)

    def text_whole(block, source, fresh):
        def step(t, carry):
            at = at_rows(t * TILE, TILE)
            loss, grad = text_terms(at, block[...], targets(source, 0, TILE, rows), rows)
            loss_acc[at, :] = loss if fresh else loss_acc[at, :] + loss
            gx_ref[at, :] = grad if fresh else gx_ref[at, :] + grad
            return carry

        lax.fori_loop(0, tiles, step, 0)

    def image_whole(block, positions, fresh):
        pos_row = jnp.concatenate([positions[g:g + 1, :] for g in range(rows // 128)], axis=1)

        def step(t, carry):
            at = at_rows(t * TILE, TILE)
            grad = image_terms(at, t * TILE, TILE, block[...], pos_row)
            gy_ref[at, :] = grad if fresh else gy_ref[at, :] + grad
            return carry

        lax.fori_loop(0, tiles, step, 0)

    def project(grad, kind, at):
        inverse = inv[kind, at, :][:, 0:1]
        unit = raw[kind, at, :].astype(jnp.float32) * inverse
        grad = grad * scale
        return (grad - unit * jnp.sum(unit * grad, axis=-1, keepdims=True)) * inverse

    def text_part(block, source, c, last=False):
        size = LAST_TILE if last else TILE
        chunk = block[at_rows(c * PART, PART), :]
        for t in range(rows // size):
            at = pl.ds(t * size, size)
            loss, grad = text_terms(at, chunk, targets(source, c * PART, size, PART), PART)
            loss_acc[at, :] += loss
            grad = gx_ref[at, :] + grad
            gx_ref[at, :] = project(grad, IMAGE, at) if last else grad

    def image_part(block, positions, c, last=False):
        size = LAST_TILE if last else TILE
        chunk = block[at_rows(c * PART, PART), :]
        pos_row = positions[pl.ds(c, 1), :]
        for t in range(rows // size):
            at = pl.ds(t * size, size)
            grad = gy_ref[at, :] + image_terms(at, t * size, size, chunk, pos_row)
            gy_ref[at, :] = project(grad, TEXT, at) if last else grad

    def finish(acc, kind):
        def step(t, carry):
            at = at_rows(t * TILE, TILE)
            acc[at, :] = project(acc[at, :], kind, at)
            return carry

        lax.fori_loop(0, tiles, step, 0)

    def losses():
        for c in range(rows // 128):
            total = jnp.sum(loss_acc[c * 128:(c + 1) * 128, :].T, axis=0, keepdims=True)
            loss_ref[c:c + 1, :] = total / rows

    near_text = lax.rem(me + n - 1, n)
    far_text = lax.rem(me + n - 2, n)

    text_whole(low.at[TEXT], me, True)
    image_whole(low.at[IMAGE], pos_ref, True)
    def steps(c, carry):
        lead(c).wait_send()

        start(jnp.where(c == 0, 0, 2 * c - 1) + IN_FLIGHT)
        lead(c).wait_recv()

        @pl.when(c == 0)
        def _():
            pos_link.wait_recv()

            @pl.when(first)
            def _():
                pos_near(places.at[FAR]).start()

            pos_near(pos_ref).wait_recv()

        pass_on(c).start()
        pass_on(c).wait_recv()
        image_part(there.at[IMAGE, core], places.at[core], c)
        text_part(there.at[TEXT, other], jnp.where(first, near_text, far_text), c)

        @pl.when(c > 0)
        def _():
            tail(c - 1).wait_send()
            start(2 * c + IN_FLIGHT)

        @pl.when(jnp.logical_and(c == parts - 1, first))
        def _():
            finish(gy_ref, TEXT)

        @pl.when(jnp.logical_and(c == parts - 1, second))
        def _():
            finish(gx_ref, IMAGE)
            losses()

        @pl.when(c > 0)
        def _():
            tail(c - 1).wait_recv()

            @pl.when(first)
            def _():
                text_part(there.at[TEXT, FAR], far_text, c - 1)

            @pl.when(second)
            def _():
                image_part(there.at[IMAGE, FAR], places.at[FAR], c - 1)

        @pl.when(c == 1)
        def _():
            whole.wait_recv()

            @pl.when(first)
            def _():
                image_whole(there.at[IMAGE, NEAR], places.at[NEAR], False)

            @pl.when(second)
            def _():
                text_whole(there.at[TEXT, NEAR], near_text, False)

        return carry

    lax.fori_loop(0, parts, steps, 0)

    tail(parts - 1).wait_send()
    whole.wait_send()
    pos_link.wait_send()
    pos_near(pos_ref).wait_send()

    def drain(c, carry):
        pass_on(c).wait_send()
        return carry

    lax.fori_loop(0, parts, drain, 0)
    tail(parts - 1).wait_recv()

    @pl.when(first)
    def _():
        text_part(there.at[TEXT, FAR], far_text, parts - 1, last=True)
        losses()

    @pl.when(second)
    def _():
        image_part(there.at[IMAGE, FAR], places.at[FAR], parts - 1, last=True)


def shards(images, texts, positive, log_scale, bias):
    rows, width = images.shape
    parts = rows // PART
    two = pltpu.VMEM((2, rows, width), jnp.bfloat16)
    column = pltpu.VMEM((rows, 128), jnp.float32)
    sems = pltpu.SemaphoreType.DMA((parts,))
    one = pltpu.SemaphoreType.DMA((1,))
    pair = pltpu.SemaphoreType.DMA((2,))
    vmem = pl.BlockSpec(memory_space=pltpu.VMEM)
    hbm = pl.BlockSpec(memory_space=pltpu.HBM)
    loss, grad_x, grad_y = pl.pallas_call(
        kernel,
        out_shape=(
            jax.ShapeDtypeStruct((rows // 128, 128), jnp.float32),
            pltpu.VMEM((rows, width), jnp.float32),
            pltpu.VMEM((rows, width), jnp.float32),
        ),
        in_specs=[hbm] * 5,
        out_specs=(vmem, vmem, vmem),
        scratch_shapes=[
            pltpu.SMEM((1,), jnp.float32),
            pltpu.SMEM((1,), jnp.float32),
            pltpu.VMEM((rows // 128, 128), jnp.int32),
            two,
            two,
            pltpu.VMEM((2, rows, 128), jnp.float32),
            pltpu.VMEM((2, 2, rows, width), jnp.bfloat16),
            pltpu.VMEM((2, rows // 128, 128), jnp.int32),
            column,
            column,
            pltpu.SemaphoreType.DMA((5,)),
            sems, sems, sems, sems, sems, sems, one, one, pair, pair,
        ],
        compiler_params=pltpu.CompilerParams(
            collective_id=0, has_side_effects=True, vmem_limit_bytes=56 * 2**20),
    )(log_scale, bias, positive.reshape(rows // 128, 128), images, texts)
    return (loss.reshape(rows), grad_x, grad_y)


def solution(mesh):
    in_specs = (
        P(("rep", "blk"), None),
        P(("rep", "blk"), None),
        P(("rep", "blk")),
        P("rep"),
        P("rep"),
    )
    out_specs = (P(("rep", "blk")), P(("rep", "blk"), None), P(("rep", "blk"), None))
    return jax.shard_map(shards, mesh=mesh, in_specs=in_specs, out_specs=out_specs, check_vma=False)
```

time: 248 us -> 96.3 us (0.39)
  waiting for transfers between devices: 176 us -> 0 us
  Pallas kernels: 0 us -> 89.5 us
  matrix products: 39.2 us -> 0 us
  starting transfers between devices: 16.7 us -> 0 us
  other arithmetic: 12.9 us -> 0 us
  local copies, waits for them, and re-layouts: 0.05 us -> 4.19 us
    ppermute x5 -> x0, waiting for transfers between devices: 176 us -> none  [from_behind(): return lax.ppermute(block, axis, route)]
    pallas_call x0 -> x1, Pallas kernels: none -> 89.5 us  [shards(): pl.pallas_call(kernel, out_shape=(jax.ShapeDtypeStruct((rows // 128, 128)...]
    dot_general x9 -> x0, matrix products: 39.2 us -> none  [the longest x3 15 us: shards(): lax.dot_general(x_low, current, (((1,), (1,)), ((), ())), preferred_eleme...]
    ppermute x5 -> x0, starting transfers between devices: 16.7 us -> none  [from_behind(): return lax.ppermute(block, axis, route)]
    mul x2 -> x0, other arithmetic: 4.95 us -> none  [the longest x1 2.48 us: shards(): (grad_x - x_unit * jnp.sum(x_unit * grad_x, axis=-1, keepdims=True)) * x_inv]
    unnamed x22 -> x5, local copies, waits for them, and re-layouts: 0.05 us -> 4.19 us
    reduce_sum x3 -> x0, other arithmetic: 3.08 us -> none  [the longest x2 2.43 us: normalize(): inverse = lax.rsqrt(jnp.sum(wide * wide, axis=-1, keepdims=True) + 1e-06)]
    add x4 -> x0, other arithmetic: 2.62 us -> none  [the longest x1 2.61 us: shards(): gathered_grad = from_behind(gathered_grad, 'blk', 1) + text_term]
  transfers between devices with their start and end apart: 5 -> 0, of which waited for: 3 -> 0; matrix products, arithmetic and copies ran while one was open for 10% -> 0% of each run, Pallas kernels for 0% -> 0%
where the time goes in v2:
time: 96.3 us; the launch traced here: 95.6 us
  Pallas kernels  89.5 us (93%)
  local copies, waits for them, and re-layouts  4.19 us (4%)
  between operations  1.93 us (2%)
    pallas_call x1, Pallas kernels, shards(): pl.pallas_call(kernel, out_shape=(jax.ShapeDtypeStruct((rows // 128, 128)...  89.5 us
    unnamed x5, local copies, waits for them, and re-layouts  4.19 us

profile of v2, /device:TPU:1, one launch (start us, length us, event | category | flops | bytes accessed | tf_op | source)
XLA Modules:
  0.0 95.6 jit_solution(9813008545078710268)
XLA Ops:
  1.9 89.5 %shard_map.76 = (f32[6,128]{1,0:T(8,128)}, f32[768,1152]{1,0:T(8,128)S(1)}, f32[768,1152]{1,0:T(8,128)S(1)}) custom-call(f32[1]{0:T(128)S(6)} %copy.13.scale_hbm, f32[1]{0:T(128)S(6)} %copy.14.bias_hbm, s32[6,128]{1,0:T(8,128)} %bitcast.2, bf16[768,1152]{1,0:T(8,128)(2,1)} %img_ref.1, bf16[768,1152]{1,0:T(8,128)(2,1)} %txt_ref.1), custom_call_target="tpu_custom_call" | custom-call | tf_op jit(solution)/shard_map/pallas_call | solution.py:321
  91.4 1.8 %copy.11 = f32[768,1152]{1,0:T(8,128)} copy(f32[768,1152]{1,0:T(8,128)S(1)} %get-tuple-element.10) | data formatting | bytes 7077888
  93.2 0.0 copy-start
  93.2 1.8 %copy.12 = f32[768,1152]{1,0:T(8,128)} copy(f32[768,1152]{1,0:T(8,128)S(1)} %get-tuple-element.11) | data formatting | bytes 7077888
  95.0 0.0 copy-done
  95.0 0.6 copy.15
Async XLA Ops:
  93.2 1.8 %copy-start = (f32[6,128]{1,0:T(8,128)S(1)}, f32[6,128]{1,0:T(8,128)}, u32[]{:S(2)}) copy-start(f32[6,128]{1,0:T(8,128)} %get-tuple-element.6) | copy-start | bytes 9220

commit v3 on v2

--- a/solution.py
+++ b/solution.py
@@ -10,7 +10,7 @@
 PART = 128
 TILE = 256
 LAST_TILE = 256
-IN_FLIGHT = 4
+IN_FLIGHT = 3
 MESH = pl.DeviceIdType.MESH
 IMAGE, TEXT = 0, 1
 FAR, NEAR = 0, 1
@@ -89,13 +89,9 @@
 
         lax.fori_loop(0, parts, step, 0)
 
-    loads[0].wait()
-    normalize(IMAGE)
-    loads[1].wait()
-    normalize(TEXT)
-    for load in loads[2:]:
+    for load in loads:
         load.wait()
-
+    normalize(core)
     pl.semaphore_wait(barrier, 3)
     def start(p):
         is_tail = jnp.logical_or(p == 2 * parts - 1, jnp.logical_and(p > 0, lax.rem(p, 2) == 0))
@@ -118,8 +114,10 @@
     def _():
         pos_near(pos_ref).start()
 
+    lax.fori_loop(0, 2, fill, 0)
+    normalize(other)
     whole.start()
-    lax.fori_loop(0, IN_FLIGHT, fill, 0)
+    lax.fori_loop(2, IN_FLIGHT, fill, 0)
 
     scale = jnp.exp(jnp.full((8, 128), scale_ref[0], jnp.float32))[0:1, 0:1]
     bias = bias_ref[0]

time: 96.3 us -> 96 us (level)
  no operation moved by 1% of the time
where the time goes in v3:
time: 96 us; the launch traced here: 95.9 us
  Pallas kernels  89.8 us (94%)
  local copies, waits for them, and re-layouts  4.19 us (4%)
  between operations  1.93 us (2%)
    pallas_call x1, Pallas kernels, shards(): pl.pallas_call(kernel, out_shape=(jax.ShapeDtypeStruct((rows // 128, 128)...  89.8 us
    unnamed x5, local copies, waits for them, and re-layouts  4.19 us

profile of v3, /device:TPU:1, one launch (start us, length us, event | category | flops | bytes accessed | tf_op | source)
XLA Modules:
  0.0 95.9 jit_solution(5292058878917781134)
XLA Ops:
  1.9 89.8 %shard_map.76 = (f32[6,128]{1,0:T(8,128)}, f32[768,1152]{1,0:T(8,128)S(1)}, f32[768,1152]{1,0:T(8,128)S(1)}) custom-call(f32[1]{0:T(128)S(6)} %copy.13.scale_hbm, f32[1]{0:T(128)S(6)} %copy.14.bias_hbm, s32[6,128]{1,0:T(8,128)} %bitcast.2, bf16[768,1152]{1,0:T(8,128)(2,1)} %img_ref.1, bf16[768,1152]{1,0:T(8,128)(2,1)} %txt_ref.1), custom_call_target="tpu_custom_call" | custom-call | tf_op jit(solution)/shard_map/pallas_call | solution.py:319
  91.7 1.8 %copy.11 = f32[768,1152]{1,0:T(8,128)} copy(f32[768,1152]{1,0:T(8,128)S(1)} %get-tuple-element.10) | data formatting | bytes 7077888
  93.5 0.0 copy-start
  93.5 1.8 %copy.12 = f32[768,1152]{1,0:T(8,128)} copy(f32[768,1152]{1,0:T(8,128)S(1)} %get-tuple-element.11) | data formatting | bytes 7077888
  95.3 0.0 copy-done
  95.3 0.6 copy.15
Async XLA Ops:
  93.5 1.8 %copy-start = (f32[6,128]{1,0:T(8,128)S(1)}, f32[6,128]{1,0:T(8,128)}, u32[]{:S(2)}) copy-start(f32[6,128]{1,0:T(8,128)} %get-tuple-element.6) | copy-start | bytes 9220

commit v4 on v3

--- a/solution.py
+++ b/solution.py
@@ -8,8 +8,8 @@
 from jax.sharding import PartitionSpec as P
 
 PART = 128
-TILE = 256
-LAST_TILE = 256
+TILE = 384
+LAST_TILE = 384
 IN_FLIGHT = 3
 MESH = pl.DeviceIdType.MESH
 IMAGE, TEXT = 0, 1

time: 96 us -> 95.3 us (level); the launches traced: 95.9 us -> 93.5 us
  Pallas kernels: 89.8 us -> 87.4 us
    pallas_call x1, Pallas kernels: 89.8 us -> 87.4 us  [shards(): pl.pallas_call(kernel, out_shape=(jax.ShapeDtypeStruct((rows // 128, 128)...]
where the time goes in v4:
time: 95.3 us; the launch traced here: 93.5 us
  Pallas kernels  87.4 us (92%)
  local copies, waits for them, and re-layouts  4.19 us (4%)
  between operations  1.93 us (2%)
    pallas_call x1, Pallas kernels, shards(): pl.pallas_call(kernel, out_shape=(jax.ShapeDtypeStruct((rows // 128, 128)...  87.4 us
    unnamed x5, local copies, waits for them, and re-layouts  4.19 us

profile of v4, /device:TPU:1, one launch (start us, length us, event | category | flops | bytes accessed | tf_op | source)
XLA Modules:
  0.0 93.5 jit_solution(13023048802761954169)
XLA Ops:
  1.9 87.4 %shard_map.76 = (f32[6,128]{1,0:T(8,128)}, f32[768,1152]{1,0:T(8,128)S(1)}, f32[768,1152]{1,0:T(8,128)S(1)}) custom-call(f32[1]{0:T(128)S(6)} %copy.13.scale_hbm, f32[1]{0:T(128)S(6)} %copy.14.bias_hbm, s32[6,128]{1,0:T(8,128)} %bitcast.2, bf16[768,1152]{1,0:T(8,128)(2,1)} %img_ref.1, bf16[768,1152]{1,0:T(8,128)(2,1)} %txt_ref.1), custom_call_target="tpu_custom_call" | custom-call | tf_op jit(solution)/shard_map/pallas_call | solution.py:319
  89.3 1.8 %copy.11 = f32[768,1152]{1,0:T(8,128)} copy(f32[768,1152]{1,0:T(8,128)S(1)} %get-tuple-element.10) | data formatting | bytes 7077888
  91.1 0.0 copy-start
  91.1 1.8 %copy.12 = f32[768,1152]{1,0:T(8,128)} copy(f32[768,1152]{1,0:T(8,128)S(1)} %get-tuple-element.11) | data formatting | bytes 7077888
  92.9 0.0 copy-done
  92.9 0.6 copy.15
Async XLA Ops:
  91.1 1.8 %copy-start = (f32[6,128]{1,0:T(8,128)S(1)}, f32[6,128]{1,0:T(8,128)}, u32[]{:S(2)}) copy-start(f32[6,128]{1,0:T(8,128)} %get-tuple-element.6) | copy-start | bytes 9220
